TPU v7x, 768 devices: a whole 4x8x12 slice. The times are simulated.
768 devices in a mesh: grp: 24 (over z, core), peer: 32 (over y, x).
Axes of the slice: x: 4, y: 8, z: 12, core: 2. Of those that a mesh axis runs over, the one named last changes fastest.
Arguments:
- descriptors: bfloat16 [196608, 256], P(('grp', 'peer'))
- cell_ids: int32 [196608], P(('grp', 'peer')), may hold values from 0 to 63, as said below
- sub_codes: int32 [196608, 32], P(('grp', 'peer')), may hold values from 0 to 255
- centroids: bfloat16 [1536, 256], P(('grp', 'peer')), may hold values from -3 to 3
- codebooks: bfloat16 [1536, 256, 256], P(('grp', 'peer')), may hold values from -6 to 6
Outputs:
- rotated: bfloat16 [196608, 256], P(('grp', 'peer'))
- rotations: float32 [1536, 256, 256], P(('grp', 'peer'))
- distortion: float32 [], replicated
Inputs may be any that keep to these rules, and one draw needn't show every extreme that they name: `cell_ids`: rows of one group name only that group's cells; cell l of a group is owned by its peer l // 2. From one device at most 8 rows name one cell and at most 10 rows name cells of one owner. In every group one cell gets exactly 8 rows from every device of the group, and its owner exactly 10 rows from every device.
All inputs are finite; a program needn't handle non-finite values.
Results may differ from a plain program's by a relative error of at most 0.0046.
Values may be sent and summed in bfloat16 or wider, within the bound.
A program may use at most 32 MiB of HBM per device.

v0:
```python
import math

import jax
import jax.numpy as jnp
from jax import lax
from jax.sharding import PartitionSpec as P

NEWTON = 3


def newton_polar(covariance):
    norm_sq = jnp.sum(covariance * covariance, axis=(-2, -1), keepdims=True)
    polar = covariance / jnp.sqrt(norm_sq + 1e-06)
    for repeat in range(NEWTON):
        gram_matrix = jnp.matmul(
            jnp.swapaxes(polar, -1, -2), polar, precision=lax.Precision.HIGHEST
        )
        polar = 1.5 * polar - 0.5 * jnp.matmul(polar, gram_matrix, precision=lax.Precision.HIGHEST)
    return polar


def rank_within(labels, label_count):
    row_total = labels.shape[0]
    block = math.gcd(row_total, 256)
    blocks = row_total // block
    onehot = (
        labels.reshape(blocks, block)[..., None]
        == jnp.arange(label_count, dtype=jnp.int32)[None, None, :]
    ).astype(jnp.bfloat16)
    positions = jnp.arange(block, dtype=jnp.int32)
    lower = (positions[:, None] > positions[None, :]).astype(jnp.bfloat16)
    inside = jnp.einsum("ij,bjg->big", lower, onehot, preferred_element_type=jnp.float32)
    totals = jnp.sum(onehot.astype(jnp.float32), axis=1)
    block_ids = jnp.arange(blocks, dtype=jnp.int32)
    block_lower = (block_ids[:, None] > block_ids[None, :]).astype(jnp.float32)
    offsets = jnp.dot(block_lower, totals, precision=lax.Precision.HIGHEST)
    counted = jnp.sum((inside + offsets[:, None, :]) * onehot.astype(jnp.float32), axis=-1)
    return counted.reshape(row_total).astype(jnp.int32)


def decode_codes(got_codes, codebooks):
    sources, owned_cells, cell_cap, sub_count = got_codes.shape
    code_count = codebooks.shape[1]
    features = codebooks.shape[2]
    width = features // sub_count
    groups = math.gcd(sub_count, 4)
    per_group = sub_count // groups
    grouped_books = codebooks.reshape(owned_cells, code_count, groups, per_group, width)
    grouped_books = jnp.moveaxis(grouped_books, 2, 0)
    grouped_codes = jnp.moveaxis(
        got_codes.reshape(sources, owned_cells, cell_cap, groups, per_group), 3, 0
    )
    code_range = jnp.arange(code_count, dtype=jnp.int32)

    def one_group(packed_pair):
        codes_part, books_part = packed_pair
        table = (codes_part[..., None] == code_range).astype(jnp.bfloat16)
        pieces = jnp.einsum(
            "ncmsk,cksf->ncmsf", table, books_part, preferred_element_type=jnp.float32
        )
        return pieces.astype(jnp.bfloat16)

    decoded = lax.map(one_group, (grouped_codes, grouped_books))
    decoded = jnp.moveaxis(decoded, 0, 3)
    return decoded.reshape(sources, owned_cells, cell_cap, features)


def process_cells(got_rows, got_codes, centroids, codebooks):
    filled = got_codes[..., 0] >= 0
    residual = jnp.where(
        filled[..., None],
        got_rows.astype(jnp.float32) - centroids[None, :, None, :].astype(jnp.float32),
        0.0,
    ).astype(jnp.bfloat16)
    rebuilt = decode_codes(got_codes, codebooks)
    covariance = jnp.einsum("ncmd,ncme->cde", residual, rebuilt, preferred_element_type=jnp.float32)
    rotations = newton_polar(covariance)
    turned = jnp.einsum(
        "ncmd,cde->ncme",
        residual,
        rotations.astype(jnp.bfloat16),
        preferred_element_type=jnp.float32,
    )
    sq_error = jnp.sum((turned - rebuilt.astype(jnp.float32)) ** 2)
    return (turned.astype(jnp.bfloat16), rotations, sq_error)


def local(descriptors, cell_ids, sub_codes, centroids, codebooks):
    peer_count = lax.axis_size("peer")
    rows_dev = descriptors.shape[0]
    features = descriptors.shape[1]
    sub_count = sub_codes.shape[1]
    owned_cells = centroids.shape[0]
    group_cells = owned_cells * peer_count
    cell_cap = 2 * rows_dev // group_cells
    padded_rows = jnp.concatenate([descriptors, jnp.zeros((1, features), jnp.bfloat16)], axis=0)
    padded_codes = jnp.concatenate([sub_codes, jnp.full((1, sub_count), -1, jnp.int32)], axis=0)
    row_ids = jnp.arange(rows_dev, dtype=jnp.int32)
    slot_index = cell_ids * cell_cap + rank_within(cell_ids, group_cells)
    slot_count = group_cells * cell_cap
    slot_source = jnp.full((slot_count,), rows_dev, jnp.int32).at[slot_index].set(row_ids)
    send_rows = padded_rows[slot_source].reshape(peer_count, owned_cells * cell_cap, features)
    send_codes = padded_codes[slot_source].reshape(peer_count, owned_cells * cell_cap, sub_count)
    got_rows, got_codes = (
        lax.all_to_all(send_rows, "peer", split_axis=0, concat_axis=0, tiled=True),
        lax.all_to_all(send_codes, "peer", split_axis=0, concat_axis=0, tiled=True),
    )
    turned, rotations, sq_error = process_cells(
        got_rows.reshape(peer_count, owned_cells, cell_cap, features),
        got_codes.reshape(peer_count, owned_cells, cell_cap, sub_count),
        centroids,
        codebooks,
    )
    returned = lax.all_to_all(
        turned.reshape(peer_count, owned_cells * cell_cap, features),
        "peer",
        split_axis=0,
        concat_axis=0,
        tiled=True,
    )
    rotated = returned.reshape(slot_count, features)[slot_index]
    devices = lax.axis_size("grp") * peer_count
    total = lax.psum(sq_error, ("grp", "peer"))
    distortion = total / float(rows_dev * devices * features)
    return (rotated, rotations, distortion)


def solution(mesh):
    in_specs = (
        P(("grp", "peer"), None),
        P(("grp", "peer")),
        P(("grp", "peer"), None),
        P(("grp", "peer"), None),
        P(("grp", "peer"), None, None),
    )
    out_specs = (P(("grp", "peer"), None), P(("grp", "peer"), None, None), P())
    return jax.shard_map(local, mesh=mesh, in_specs=in_specs, out_specs=out_specs, check_vma=False)
```

profile of v0, /device:TPU:1, one launch (start us, length us, event | category | flops | bytes accessed | tf_op | source)
XLA Modules:
  0.0 180.3 jit_solution(1401054837092436998)
XLA Ops:
  0.6 0.9 copy.64
  1.5 0.8 convert_reduce_fusion
  2.3 1.0 fusion.16
  3.3 0.7 compare_select_fusion.1
  4.0 1.4 scatter_custom_fusion
  5.5 0.0 copy-start.1
  5.5 1.0 gather_fusion
  6.5 0.0 copy-start.2
  6.5 0.8 reshape.155
  7.3 10.5 %all-to-all-start = ((s32[32,1,512]{2,1,0:T(1,128)}), s32[32,1,512]{2,1,0:T(1,128)S(1)}, u32[]{:S(2)}, u32[]{:S(2)}) async-start(s32[32,1,512]{2,1,0:T(1,128)} %reshape.155), calls=%async_computation | async-start | bytes 131072 | tf_op jit(solution)/shard_map/all_to_all | solution.py:106
  17.9 0.0 copy-done.1
  17.9 0.1 copy.67
  18.0 0.0 copy-done.2
  18.0 0.0 copy-start.3
  18.0 2.6 %gather_fusion.1 = bf16[512,256]{1,0:T(8,128)(2,1)} fusion(bf16[257,256]{1,0:T(8,128)(2,1)S(1)} %concatenate.7, s32[1024]{0:T(1024)S(1)} %pad_clamp_fusion.1), kind=kCustom, calls=%fused_computation.1 | custom fusion | bytes 526336 | tf_op jit(solution)/shard_map/gather | solution.py:102
  20.6 0.0 copy-done.3
  20.6 6.0 %all-to-all-done = s32[32,1,512]{2,1,0:T(1,128)S(1)} async-done(((s32[32,1,512]{2,1,0:T(1,128)}), s32[32,1,512]{2,1,0:T(1,128)S(1)}, u32[]{:S(2)}, u32[]{:S(2)}) %all-to-all-start) | async-done | bytes 65568 | tf_op jit(solution)/shard_map/all_to_all | solution.py:106
  26.7 3.9 %all-to-all-start.1 = ((bf16[32,16,256]{2,1,0:T(8,128)(2,1)}), bf16[32,16,256]{2,1,0:T(8,128)(2,1)S(1)}, u32[]{:S(2)}, u32[]{:S(2)}) async-start(bf16[32,16,256]{2,1,0:T(8,128)(2,1)} %bitcast.5), calls=%async_computation.1 | async-start | bytes 524288 | tf_op jit(solution)/shard_map/all_to_all | solution.py:105
  30.5 0.5 broadcast.94
  31.1 0.8 reduce.2
  31.9 0.1 reshape.156
  32.0 0.2 copy.68
  32.1 7.4 %while.11 = (s32[]{:T(128)}, bf16[4,32,2,8,8,8]{1,5,3,4,2,0:T(8,128)(2,1)S(1)}, bf16[4,2,256,8,8]{2,4,3,0,1:T(8,128)(2,1)S(1)}, s32[4,32,2,8,8]{1,4,0,3,2:T(8,128)S(1)}, s32[]{:T(128)}) while((s32[]{:T(128)}, bf16[4,32,2,8,8,8]{1,5,3,4,2,0:T(8,128)(2,1)S(1)}, bf16[4,2,256,8,8]{2,4,3,0,1:T(8,128)(2,1)S(1)}, ...), condition=%wide.region_4.5_spmd.clone, body=%wide.region_3.4_spmd.clone.sunk | while | flops 17858560 | bytes 459849 | solution.py:63
  32.2 1.8 fusion.43
  34.1 1.8 fusion.43
  35.9 1.8 fusion.43
  37.8 1.8 fusion.43
  39.6 0.3 copy.71
  39.9 0.3 copy.77
  40.2 0.2 copy.87
  40.4 0.7 all-to-all-done.1
  41.1 0.1 copy.66
  41.2 0.8 multiply_reduce_fusion.1
  42.0 1.2 fusion.20
  43.2 0.7 fusion.12
  43.9 1.1 fusion.28
  45.0 0.7 fusion.11
  45.7 1.1 fusion.29
  46.7 0.7 fusion.10
  47.4 0.0 copy-start
  47.4 0.9 multiply_reduce_fusion
  48.4 0.8 copy.76
  49.2 0.0 copy-done
  49.2 8.5 %all-to-all-start.2 = ((bf16[32,16,256]{2,1,0:T(8,128)(2,1)}), bf16[32,16,256]{2,1,0:T(8,128)(2,1)S(1)}, u32[]{:S(2)}, u32[]{:S(2)}) async-start(bf16[32,16,256]{2,1,0:T(8,128)(2,1)} %copy.76), calls=%async_computation.2 | async-start | bytes 524288 | tf_op jit(solution)/shard_map/all_to_all | solution.py:114
  57.7 118.9 %psum.7 = f32[]{:T(128)} all-reduce(f32[]{:T(128)} %get-tuple-element.69), channel_id=1, replica_groups=mesh['grp'=24,'peer'=32] {'grp','peer'}, use_global_device_ids=true, to_apply=%region_7.8 | all-reduce | flops 1 | bytes 8 | tf_op jit(solution)/shard_map/psum | solution.py:123
  177.3 0.0 all-to-all-done.2
  177.3 1.8 %gather_fusion.2 = bf16[256,256]{1,0:T(8,128)(2,1)} fusion(bf16[512,256]{1,0:T(8,128)(2,1)S(1)} %bitcast.80, s32[1024]{0:T(1024)S(1)} %pad_clamp_fusion), kind=kCustom, calls=%fused_computation.2 | custom fusion | bytes 263168 | tf_op jit(solution)/shard_map/gather | solution.py:121
  (19 shorter events, 0.2 us)
Async XLA Ops:
  5.5 12.4 %copy-start.1 = (bf16[2,256,256]{2,1,0:T(8,128)(2,1)S(1)}, bf16[2,256,256]{2,1,0:T(8,128)(2,1)}, u32[]{:S(2)}) copy-start(bf16[2,256,256]{2,1,0:T(8,128)(2,1)} %param.11) | copy-start | bytes 786436
  6.5 11.5 %copy-start.2 = (bf16[256,256]{1,0:T(8,128)(2,1)S(1)}, bf16[256,256]{1,0:T(8,128)(2,1)}, u32[]{:S(2)}) copy-start(bf16[256,256]{1,0:T(8,128)(2,1)} %param.7) | copy-start | bytes 393220
  7.3 19.3 %all-to-all-start = ((s32[32,1,512]{2,1,0:T(1,128)}), s32[32,1,512]{2,1,0:T(1,128)S(1)}, u32[]{:S(2)}, u32[]{:S(2)}) async-start(s32[32,1,512]{2,1,0:T(1,128)} %reshape.155), calls=%async_computation | async-start | bytes 131072 | tf_op jit(solution)/shard_map/all_to_all | solution.py:106
  18.0 2.6 %copy-start.3 = (bf16[2,256]{1,0:T(2,128)(2,1)S(1)}, bf16[2,256]{1,0:T(2,128)(2,1)}, u32[]{:S(2)}) copy-start(bf16[2,256]{1,0:T(2,128)(2,1)} %param.10) | copy-start | bytes 3076
  26.7 14.5 %all-to-all-start.1 = ((bf16[32,16,256]{2,1,0:T(8,128)(2,1)}), bf16[32,16,256]{2,1,0:T(8,128)(2,1)S(1)}, u32[]{:S(2)}, u32[]{:S(2)}) async-start(bf16[32,16,256]{2,1,0:T(8,128)(2,1)} %bitcast.5), calls=%async_computation.1 | async-start | bytes 524288 | tf_op jit(solution)/shard_map/all_to_all | solution.py:105
  47.4 1.8 copy-start
  49.2 128.1 %all-to-all-start.2 = ((bf16[32,16,256]{2,1,0:T(8,128)(2,1)}), bf16[32,16,256]{2,1,0:T(8,128)(2,1)S(1)}, u32[]{:S(2)}, u32[]{:S(2)}) async-start(bf16[32,16,256]{2,1,0:T(8,128)(2,1)} %copy.76), calls=%async_computation.2 | async-start | bytes 524288 | tf_op jit(solution)/shard_map/all_to_all | solution.py:114
where the time goes:
time: 181 us; the launch traced here: 180 us
  blocking collectives  119 us (66%)
  starting transfers between devices  22.9 us (13%)
  matrix products  15.3 us (8%)
  local copies, waits for them, and re-layouts  11.3 us (6%)
  waiting for transfers between devices  6.78 us (4%)
  between operations  2.66 us (1%)
  other arithmetic  2.32 us (1%)
    psum x1, blocking collectives, local(): total = lax.psum(sq_error, ('grp', 'peer'))  119 us
    all_to_all x1, starting transfers between devices, local(): lax.all_to_all(send_codes, 'peer', split_axis=0, concat_axis=0, tiled=True)  10.5 us
    all_to_all x1, starting transfers between devices, local(): lax.all_to_all(turned.reshape(peer_count, owned_cells * cell_cap, feature...  8.47 us
    dot_general x4, matrix products, one_group(): jnp.einsum('ncmsk,cksf->ncmsf', table, books_part, preferred_element_type...  7.18 us
    all_to_all x1, waiting for transfers between devices, local(): lax.all_to_all(send_codes, 'peer', split_axis=0, concat_axis=0, tiled=True)  6.03 us
    all_to_all x1, starting transfers between devices, local(): lax.all_to_all(send_rows, 'peer', split_axis=0, concat_axis=0, tiled=True)  3.87 us
  transfers between devices with their start and end apart: 3, of which 2 were waited for; matrix products, arithmetic and copies ran while one was open for 7% of the time, Pallas kernels for 0%

commit v1 on v0

v1 whole, which is shorter than its diff:
```python
import jax
import jax.numpy as jnp
from jax import lax
from jax.experimental import pallas as pl
from jax.experimental.pallas import tpu as pltpu
from jax.sharding import PartitionSpec as P

MESH = pl.DeviceIdType.MESH
NEWTON = 3
D = 256
SUB = 32
CODES = 256
ROWS_DEV = 256
SLOT = 16
CODE_ROW = 10
X_SIZE, Y_SIZE = 4, 8
PEERS = X_SIZE * Y_SIZE
CHUNK = 8
CHUNKS = PEERS // CHUNK
CROWS = CHUNK * SLOT
F32, BF16, I32 = jnp.float32, jnp.bfloat16, jnp.int32


def nn(a, b):
    return jnp.dot(a, b, preferred_element_type=F32)


def nt(a, b):
    return lax.dot_general(a, b, (((1,), (1,)), ((), ())), preferred_element_type=F32)


def iota(shape, dim):
    return lax.broadcasted_iota(I32, shape, dim)


def kernel(
    groups,
    desc_ref,
    cell_ref,
    code_ref,
    cent_ref,
    book_ref,
    rotated_ref,
    rot_ref,
    dist_ref,
    send,
    got,
    back,
    ret,
    table,
    rebuilt,
    resid,
    cov,
    perm_t,
    err_mine,
    err_peer,
    err_sum,
    err_grp,
    out_sem,
    in_sem,
    back_sem,
    ret_sem,
    ep_out,
    ep_in,
    eg_out,
    eg_in,
):
    me_g = lax.axis_index("grp")
    me_p = lax.axis_index("peer")
    my_y, my_x = me_p // X_SIZE, me_p % X_SIZE

    def ahead(delta):
        to_y = (my_y + delta // X_SIZE) % Y_SIZE
        to_x = (my_x + delta % X_SIZE) % X_SIZE
        return (me_g, to_y * X_SIZE + to_x)

    def behind(delta):
        to_y = (my_y + Y_SIZE - delta // X_SIZE) % Y_SIZE
        to_x = (my_x + X_SIZE - delta % X_SIZE) % X_SIZE
        return (me_g, to_y * X_SIZE + to_x)

    def level(step):
        return ((me_g + step) % groups, me_p)

    barrier = pltpu.get_barrier_semaphore()

    def greet_peer(delta, carry):
        pl.semaphore_signal(barrier, inc=1, device_id=ahead(delta), device_id_type=MESH)
        return carry

    def greet_level(step, carry):
        pl.semaphore_signal(barrier, inc=1, device_id=level(step), device_id_type=MESH)
        return carry

    lax.fori_loop(1, PEERS, greet_peer, 0)
    lax.fori_loop(1, groups, greet_level, 0)

    cell = cell_ref[...]
    owner = cell >> 1
    rel = (((owner >> 2) - my_y) & (Y_SIZE - 1)) * X_SIZE + (((owner & 3) - my_x) & (X_SIZE - 1))
    hot = iota((PEERS, ROWS_DEV), 0) == rel
    earlier = (iota((ROWS_DEV, ROWS_DEV), 0) < iota((ROWS_DEV, ROWS_DEV), 1)).astype(F32).astype(BF16)
    count = nn(hot.astype(F32).astype(BF16), earlier)
    rank = jnp.sum(jnp.where(hot, count, 0.0), axis=0, keepdims=True).astype(I32)
    slot = rel * SLOT + rank
    code_slot = rel * SLOT + CODE_ROW + (rank >> 3)
    position = iota((PEERS * SLOT, ROWS_DEV), 0)
    place = (position == slot).astype(F32).astype(BF16)
    code_place = (position == code_slot).astype(F32).astype(BF16)
    code = code_ref[...] + 1
    signed = jnp.where((cell & 1) == 1, -code, code).astype(F32)
    spread = jnp.concatenate(
        [jnp.where((rank & 7) == k, signed, 0.0) for k in range(8)], axis=0
    ).astype(BF16)
    packed = nn(place, desc_ref[...]) + nt(code_place, spread)
    send[...] = packed.astype(BF16).reshape(PEERS, SLOT, D)

    pl.semaphore_wait(barrier, PEERS - 1 + groups - 1)

    def out_copy(delta):
        return pltpu.make_async_remote_copy(
            src_ref=send.at[delta],
            dst_ref=got.at[delta],
            send_sem=out_sem.at[delta],
            recv_sem=in_sem.at[delta],
            device_id=ahead(delta),
            device_id_type=MESH,
        )

    def start_out(delta, carry):
        out_copy(delta).start()
        return carry

    lax.fori_loop(1, PEERS, start_out, 0)
    got[0] = send[0]

    for c in range(2):
        table[c] = book_ref[c].astype(F32).T
    perm_t[...] = place.astype(F32).T.astype(BF16)
    cov[...] = jnp.zeros_like(cov)
    cent = cent_ref[...].astype(F32)

    row = iota((CROWS, CROWS), 0)
    col = iota((CROWS, CROWS), 1)
    used = (row % SLOT) < CODE_ROW
    pick = (
        (row // SLOT == col // SLOT)
        & (col % SLOT == CODE_ROW + (row % SLOT) // 8)
        & used
    ).astype(F32).astype(BF16)
    lane = iota((CROWS, D), 1)
    own_lane = (lane // SUB) == (iota((CROWS, D), 0) % SLOT) % 8
    fold = (iota((SUB, D), 1) % SUB == iota((SUB, D), 0)).astype(F32).astype(BF16)
    first = (iota((D, 128), 0) % SUB == 0).astype(F32).astype(BF16)

    def wait_in(delta, carry):
        out_copy(delta).wait_recv()
        return carry

    def decode(chunk, carry):
        lax.fori_loop(jnp.maximum(chunk * CHUNK, 1), chunk * CHUNK + CHUNK, wait_in, 0)
        rows = got[pl.ds(chunk * CHUNK, CHUNK)].reshape(CROWS, D)
        codes = jnp.where(own_lane, nn(pick, rows), 0.0).astype(BF16)
        code_t = nt(fold, codes)
        code_col = nn(codes, first)
        rows = rows.astype(F32)
        keep = [code_col > 0.0, code_col < 0.0]
        which = (jnp.abs(code_t) - 1.0).astype(I32)
        parts = [[], []]
        for s in range(SUB):
            index = jnp.broadcast_to(which[s : s + 1], (8, CROWS))
            sign = jnp.broadcast_to(code_t[s : s + 1], (8, CROWS))
            near = index & 127
            for c in range(2):
                low = table[c, 8 * s : 8 * s + 8, 0:128]
                high = table[c, 8 * s : 8 * s + 8, 128:256]
                low = jnp.take_along_axis(low, near, axis=1, mode="promise_in_bounds")
                high = jnp.take_along_axis(high, near, axis=1, mode="promise_in_bounds")
                value = jnp.where(index < 128, low, high)
                valid = sign > 0.0 if c == 0 else sign < 0.0
                parts[c].append(jnp.where(valid, value, 0.0))
        rebuilt_t = [jnp.concatenate(p, axis=0) for p in parts]
        rebuilt[chunk] = (rebuilt_t[0] + rebuilt_t[1]).T
        for c in range(2):
            residual = (rows - cent[c : c + 1]).astype(BF16)
            cov[c] += nn(rebuilt_t[c].astype(BF16), residual)
            both = jnp.concatenate([keep[c], keep[c]], axis=1)
            resid[c, chunk] = jnp.where(both, residual.astype(F32), 0.0).astype(BF16)
        return carry

    lax.fori_loop(0, CHUNKS, decode, 0)

    polar = []
    for c in range(2):
        norm = jnp.sum(cov[c] * cov[c], keepdims=True)
        polar.append(cov[c] * lax.rsqrt(norm + 1e-06))
    for _ in range(NEWTON):
        small = [q.astype(BF16) for q in polar]
        gram = [nt(q, q).astype(BF16) for q in small]
        polar = [1.5 * q - 0.5 * nn(g, b) for q, g, b in zip(polar, gram, small)]
    turn = [q.astype(BF16) for q in polar]

    def turn_chunk(chunk, total):
        turned = nt(resid[0, chunk], turn[0]) + nt(resid[1, chunk], turn[1])
        off = turned - rebuilt[chunk]
        back[pl.ds(chunk * CHUNK, CHUNK)] = turned.astype(BF16).reshape(CHUNK, SLOT, D)
        return total + jnp.sum(off * off, axis=0, keepdims=True)

    total = jnp.zeros((1, D), F32)
    for chunk in range(CHUNKS):
        total = turn_chunk(chunk, total)
    err_mine[...] = total[:, :128] + total[:, 128:]
    err_peer[0] = err_mine[...]

    def err_copy(delta):
        return pltpu.make_async_remote_copy(
            src_ref=err_mine,
            dst_ref=err_peer.at[delta],
            send_sem=ep_out.at[delta],
            recv_sem=ep_in.at[delta],
            device_id=ahead(delta),
            device_id_type=MESH,
        )

    def back_copy(delta):
        return pltpu.make_async_remote_copy(
            src_ref=back.at[delta],
            dst_ref=ret.at[delta],
            send_sem=back_sem.at[delta],
            recv_sem=ret_sem.at[delta],
            device_id=behind(delta),
            device_id_type=MESH,
        )

    def grp_copy(step):
        return pltpu.make_async_remote_copy(
            src_ref=err_sum,
            dst_ref=err_grp.at[step],
            send_sem=eg_out.at[step],
            recv_sem=eg_in.at[step],
            device_id=level(step),
            device_id_type=MESH,
        )

    def loop(stop, act):
        def body(index, carry):
            act(index)
            return carry

        lax.fori_loop(1, stop, body, 0)

    loop(PEERS, lambda d: err_copy(d).start())
    loop(PEERS, lambda d: back_copy(d).start())
    ret[0] = back[0]
    for c in range(2):
        rot_ref[c] = polar[c].T

    loop(PEERS, lambda d: err_copy(d).wait_recv())
    err_sum[...] = jnp.sum(err_peer[...], axis=0)
    err_grp[0] = err_sum[...]
    loop(groups, lambda s: grp_copy(s).start())

    loop(PEERS, lambda d: back_copy(d).wait_recv())
    rotated_ref[...] = nn(perm_t[...], ret[...].reshape(PEERS * SLOT, D)).astype(BF16)

    loop(groups, lambda s: grp_copy(s).wait_recv())
    sums = jnp.sum(err_grp[...], axis=0)
    scale = 1.0 / (ROWS_DEV * PEERS * groups * D)
    dist_ref[...] = jnp.sum(sums, axis=1, keepdims=True) * scale

    loop(PEERS, lambda d: out_copy(d).wait_send())
    loop(PEERS, lambda d: err_copy(d).wait_send())
    loop(PEERS, lambda d: back_copy(d).wait_send())
    loop(groups, lambda s: grp_copy(s).wait_send())


def solution(mesh):
    groups = mesh.shape["grp"]

    def local(descriptors, cell_ids, sub_codes, centroids, codebooks):
        rotated, rotations, distortion = pl.pallas_call(
            lambda *refs: kernel(groups, *refs),
            out_shape=(
                jax.ShapeDtypeStruct((ROWS_DEV, D), BF16),
                jax.ShapeDtypeStruct((2, D, D), F32),
                jax.ShapeDtypeStruct((1, 1), F32),
            ),
            in_specs=[pl.BlockSpec(memory_space=pltpu.VMEM)] * 5,
            out_specs=(pl.BlockSpec(memory_space=pltpu.VMEM),) * 3,
            scratch_shapes=[
                pltpu.VMEM((PEERS, SLOT, D), BF16),
                pltpu.VMEM((PEERS, SLOT, D), BF16),
                pltpu.VMEM((PEERS, SLOT, D), BF16),
                pltpu.VMEM((PEERS, SLOT, D), BF16),
                pltpu.VMEM((2, D, CODES), F32),
                pltpu.VMEM((CHUNKS, CROWS, D), F32),
                pltpu.VMEM((2, CHUNKS, CROWS, D), BF16),
                pltpu.VMEM((2, D, D), F32),
                pltpu.VMEM((ROWS_DEV, PEERS * SLOT), BF16),
                pltpu.VMEM((1, 128), F32),
                pltpu.VMEM((PEERS, 1, 128), F32),
                pltpu.VMEM((1, 128), F32),
                pltpu.VMEM((groups, 1, 128), F32),
                pltpu.SemaphoreType.DMA((PEERS,)),
                pltpu.SemaphoreType.DMA((PEERS,)),
                pltpu.SemaphoreType.DMA((PEERS,)),
                pltpu.SemaphoreType.DMA((PEERS,)),
                pltpu.SemaphoreType.DMA((PEERS,)),
                pltpu.SemaphoreType.DMA((PEERS,)),
                pltpu.SemaphoreType.DMA((groups,)),
                pltpu.SemaphoreType.DMA((groups,)),
            ],
            compiler_params=pltpu.CompilerParams(
                collective_id=0, has_side_effects=True, vmem_limit_bytes=32 * 1024 * 1024
            ),
        )(descriptors, cell_ids.reshape(1, ROWS_DEV), sub_codes.T, centroids, codebooks)
        return rotated, rotations, distortion.reshape(())

    rows = P(("grp", "peer"), None)
    cells = P(("grp", "peer"), None, None)
    return jax.shard_map(
        local,
        mesh=mesh,
        in_specs=(rows, P(("grp", "peer")), rows, rows, cells),
        out_specs=(rows, cells, P()),
        check_vma=False,
    )
```

time: 181 us -> 57.2 us (0.32)
  blocking collectives: 119 us -> 0 us
  Pallas kernels: 0 us -> 49.8 us
  starting transfers between devices: 22.9 us -> 0 us
  matrix products: 15.3 us -> 0 us
  waiting for transfers between devices: 6.78 us -> 0 us
  local copies, waits for them, and re-layouts: 11.3 us -> 4.74 us
  other arithmetic: 2.32 us -> 0 us
    psum x1 -> x0, blocking collectives: 119 us -> none  [local(): total = lax.psum(sq_error, ('grp', 'peer'))]
    pallas_call x0 -> x1, Pallas kernels: none -> 49.8 us  [local(): pl.pallas_call(lambda *refs: kernel(groups, *refs), out_shape=(jax.ShapeD...]
    all_to_all x3 -> x0, starting transfers between devices: 22.9 us -> none  [the longest x1 10.5 us: local(): lax.all_to_all(send_codes, 'peer', split_axis=0, concat_axis=0, tiled=True)]
    dot_general x13 -> x0, matrix products: 15.3 us -> none  [the longest x4 7.18 us: one_group(): jnp.einsum('ncmsk,cksf->ncmsf', table, books_part, preferred_element_type...]
    all_to_all x3 -> x0, waiting for transfers between devices: 6.78 us -> none  [the longest x1 6.03 us: local(): lax.all_to_all(send_codes, 'peer', split_axis=0, concat_axis=0, tiled=True)]
    gather x3 -> x0, local copies, waits for them, and re-layouts: 5.42 us -> none  [the longest x1 2.58 us: local(): padded_rows[slot_source]]
    unnamed x13 -> x12, local copies, waits for them, and re-layouts: 2.1 us -> 4.74 us
  transfers between devices with their start and end apart: 3 -> 0, of which waited for: 2 -> 0; matrix products, arithmetic and copies ran while one was open for 7% -> 0% of each run, Pallas kernels for 0% -> 0%
where the time goes in v1:
time: 57.2 us; the launch traced here: 56.9 us
  Pallas kernels  49.8 us (87%)
  local copies, waits for them, and re-layouts  4.74 us (8%)
  between operations  2.35 us (4%)
    pallas_call x1, Pallas kernels, local(): pl.pallas_call(lambda *refs: kernel(groups, *refs), out_shape=(jax.ShapeD...  49.8 us
    unnamed x12, local copies, waits for them, and re-layouts  4.74 us

profile of v1, /device:TPU:1, one launch (start us, length us, event | category | flops | bytes accessed | tf_op | source)
XLA Modules:
  0.0 56.9 jit_solution(14146974745554178044)
XLA Ops:
  0.6 0.0 copy-start.4
  0.6 0.0 copy-start.3
  0.7 0.7 %copy-done.4 = bf16[2,256]{1,0:T(2,128)(2,1)S(1)} copy-done((bf16[2,256]{1,0:T(2,128)(2,1)S(1)}, bf16[2,256]{1,0:T(2,128)(2,1)}, u32[]{:S(2)}) %copy-start.4) | copy-done | bytes 1048
  1.3 0.0 copy-done.3
  1.3 0.0 copy-start
  1.3 0.9 %copy-done = bf16[2,256,256]{2,1,0:T(8,128)(2,1)S(1)} copy-done((bf16[2,256,256]{2,1,0:T(8,128)(2,1)S(1)}, bf16[2,256,256]{2,1,0:T(8,128)(2,1)}, u32[]{:S(2)}) %copy-start) | copy-done | bytes 262168
  2.3 0.0 copy-start.1
  2.3 0.9 %copy-done.1 = bf16[256,256]{1,0:T(8,128)(2,1)S(1)} copy-done((bf16[256,256]{1,0:T(8,128)(2,1)S(1)}, bf16[256,256]{1,0:T(8,128)(2,1)}, u32[]{:S(2)}) %copy-start.1) | copy-done | bytes 131096
  3.2 0.0 copy-start.2
  3.2 0.8 %copy-done.2 = s32[256,32]{0,1:T(8,128)S(1)} copy-done((s32[256,32]{0,1:T(8,128)S(1)}, s32[256,32]{0,1:T(8,128)}, u32[]{:S(2)}) %copy-start.2) | copy-done | bytes 32792
  3.9 49.8 %shard_map.76 = (bf16[256,256]{1,0:T(8,128)(2,1)S(1)}, f32[2,256,256]{2,1,0:T(8,128)S(1)}, f32[1,1]{1,0:T(1,128)}) custom-call(bf16[256,256]{1,0:T(8,128)(2,1)S(1)} %copy-done.1, s32[1,256]{1,0:T(1,128)S(1)} %bitcast.4, s32[32,256]{1,0:T(8,128)S(1)} %bitcast.3, bf16[2,256]{1,0:T(2,128)(2,1)S(1)} %copy-done.4, bf16[2,256,256]{2,1,0:T(8,128)(2,1)S(1)} %copy-done), custom_call_target="tpu_custom_call" | custom-call | tf_op jit(solution)/shard_map/pallas_call | solution.py:281
  53.8 0.7 %copy.11 = bf16[256,256]{1,0:T(8,128)(2,1)} copy(bf16[256,256]{1,0:T(8,128)(2,1)S(1)} %get-tuple-element.12) | data formatting | bytes 262144
  54.4 0.8 %copy.12 = f32[2,256,256]{2,1,0:T(8,128)} copy(f32[2,256,256]{2,1,0:T(8,128)S(1)} %get-tuple-element.13) | data formatting | bytes 1048576
Async XLA Ops:
  0.6 0.7 %copy-start.4 = (bf16[2,256]{1,0:T(2,128)(2,1)S(1)}, bf16[2,256]{1,0:T(2,128)(2,1)}, u32[]{:S(2)}) copy-start(bf16[2,256]{1,0:T(2,128)(2,1)} %refs_3_.1) | copy-start | bytes 3076
  0.6 0.7 %copy-start.3 = (s32[256]{0:T(256)S(1)}, s32[256]{0:T(256)}, u32[]{:S(2)}) copy-start(s32[256]{0:T(256)} %param.6) | copy-start | bytes 3076
  1.3 0.9 %copy-start = (bf16[2,256,256]{2,1,0:T(8,128)(2,1)S(1)}, bf16[2,256,256]{2,1,0:T(8,128)(2,1)}, u32[]{:S(2)}) copy-start(bf16[2,256,256]{2,1,0:T(8,128)(2,1)} %refs_4_.1) | copy-start | bytes 786436
  2.3 0.9 %copy-start.1 = (bf16[256,256]{1,0:T(8,128)(2,1)S(1)}, bf16[256,256]{1,0:T(8,128)(2,1)}, u32[]{:S(2)}) copy-start(bf16[256,256]{1,0:T(8,128)(2,1)} %refs_0_.1) | copy-start | bytes 393220
  3.2 0.8 %copy-start.2 = (s32[256,32]{0,1:T(8,128)S(1)}, s32[256,32]{0,1:T(8,128)}, u32[]{:S(2)}) copy-start(s32[256,32]{0,1:T(8,128)} %param.7) | copy-start | bytes 98308

commit v2 on v1

v2 whole, which is shorter than its diff:
```python
import jax
import jax.numpy as jnp
from jax import lax
from jax.experimental import pallas as pl
from jax.experimental.pallas import tpu as pltpu
from jax.sharding import PartitionSpec as P

MESH = pl.DeviceIdType.MESH
NEWTON = 3
D = 256
HALF = 128
SUB = 32
CODES = 256
ROWS_DEV = 256
OWN = 10
X_SIZE, Y_SIZE = 4, 8
PEERS = X_SIZE * Y_SIZE
MSG = 24
SLOT = 16
CHUNK = 8
CHUNKS = PEERS // CHUNK
CROWS = CHUNK * SLOT
CMSG = CHUNK * MSG
F32, BF16, I32 = jnp.float32, jnp.bfloat16, jnp.int32


def hops(delta):
    y, x = delta // X_SIZE, delta % X_SIZE
    return min(y, Y_SIZE - y) + min(x, X_SIZE - x)


FAR_FIRST = sorted(range(1, PEERS), key=lambda delta: -hops(delta))
CHUNK_ORDER = (2, 1, 3, 0)


def nn(a, b):
    return jnp.dot(a, b, preferred_element_type=F32)


def nt(a, b):
    return lax.dot_general(a, b, (((1,), (1,)), ((), ())), preferred_element_type=F32)


def iota(shape, dim):
    return lax.broadcasted_iota(I32, shape, dim)


def hot(mask):
    return mask.astype(F32).astype(BF16)


def loop(start, stop, act):
    def body(index, carry):
        act(index)
        return carry

    lax.fori_loop(start, stop, body, 0)


def kernel(
    groups,
    desc_hbm,
    cell_hbm,
    code_hbm,
    cent_hbm,
    book_hbm,
    rotated_ref,
    rot_ref,
    dist_ref,
    desc_ref,
    cell_ref,
    code_ref,
    cent_ref,
    book_ref,
    load_sem,
    send,
    got,
    back,
    ret,
    table,
    rebuilt,
    resid,
    cov,
    perm_t,
    err_mine,
    err_grp,
    err_sum,
    err_peer,
    out_sem,
    in_sem,
    back_sem,
    ret_sem,
    eg_out,
    eg_in,
    ep_out,
    ep_in,
):
    me_g = lax.axis_index("grp")
    me_p = lax.axis_index("peer")
    my_y, my_x = me_p // X_SIZE, me_p % X_SIZE
    levels = sorted(range(1, groups), key=lambda step: abs(2 * step - groups))

    def ahead(delta):
        to_y = (my_y + delta // X_SIZE) % Y_SIZE
        to_x = (my_x + delta % X_SIZE) % X_SIZE
        return (me_g, to_y * X_SIZE + to_x)

    def behind(delta):
        to_y = (my_y + Y_SIZE - delta // X_SIZE) % Y_SIZE
        to_x = (my_x + X_SIZE - delta % X_SIZE) % X_SIZE
        return (me_g, to_y * X_SIZE + to_x)

    def level(step):
        return ((me_g + step) % groups, me_p)

    barrier = pltpu.get_barrier_semaphore()
    for delta in FAR_FIRST:
        pl.semaphore_signal(barrier, inc=1, device_id=ahead(delta), device_id_type=MESH)
    for step in levels:
        pl.semaphore_signal(barrier, inc=1, device_id=level(step), device_id_type=MESH)

    loads = [
        pltpu.make_async_copy(src, dst, load_sem.at[i])
        for i, (src, dst) in enumerate(
            [
                (cell_hbm, cell_ref),
                (code_hbm, code_ref),
                (desc_hbm, desc_ref),
                (cent_hbm, cent_ref),
                (book_hbm, book_ref),
            ]
        )
    ]
    for load in loads:
        load.start()

    loads[0].wait()
    cell = cell_ref[...]
    owner = cell >> 1
    rel = (((owner >> 2) - my_y) & (Y_SIZE - 1)) * X_SIZE + (((owner & 3) - my_x) & (X_SIZE - 1))
    owned = iota((PEERS, ROWS_DEV), 0) == rel
    earlier = hot(iota((ROWS_DEV, ROWS_DEV), 0) < iota((ROWS_DEV, ROWS_DEV), 1))
    count = nn(hot(owned), earlier)
    rank = jnp.sum(jnp.where(owned, count, 0.0), axis=0, keepdims=True).astype(I32)
    low = rel * MSG + rank
    position = iota((PEERS * MSG, ROWS_DEV), 0)
    loads[1].wait()
    code = code_ref[...] + 1
    signed = jnp.where((cell & 1) == 1, -code, code).astype(F32)
    spread = jnp.concatenate(
        [jnp.where((rank & 3) == k, signed, 0.0) for k in range(4)], axis=0
    ).astype(BF16)
    loads[2].wait()
    packed = (
        nn(hot(position == low), desc_ref[:, :HALF])
        + nn(hot(position == low + OWN), desc_ref[:, HALF:])
        + nt(hot(position == rel * MSG + 2 * OWN + (rank >> 2)), spread)
    )
    send[...] = packed.astype(BF16).reshape(PEERS, MSG, HALF)

    pl.semaphore_wait(barrier, PEERS - 1 + groups - 1)

    def out_copy(delta):
        return pltpu.make_async_remote_copy(
            src_ref=send.at[delta],
            dst_ref=got.at[delta],
            send_sem=out_sem.at[delta],
            recv_sem=in_sem.at[delta],
            device_id=ahead(delta),
            device_id_type=MESH,
        )

    for delta in FAR_FIRST:
        out_copy(delta).start()
    got[0] = send[0]

    place = rel * SLOT + rank
    place_col = jnp.broadcast_to(place.astype(F32), (8, ROWS_DEV)).T[:, :1].astype(I32)
    perm_t[...] = hot(iota((ROWS_DEV, PEERS * SLOT), 1) == place_col)
    loads[3].wait()
    loads[4].wait()
    for c in range(2):
        table[c] = book_ref[c].astype(F32).T
    cov[...] = jnp.zeros_like(cov)
    cent = cent_ref[...].astype(F32)

    row = iota((CROWS, CMSG), 0)
    source, slot = row // SLOT, row % SLOT
    col = iota((CROWS, CMSG), 1)
    col_source, col_row = col // MSG, col % MSG
    same = (source == col_source) & (slot < OWN)
    pick_low = hot(same & (col_row == slot))
    pick_high = hot(same & (col_row == slot + OWN))
    pick_code = hot(same & (col_row == 2 * OWN + (slot >> 2)))
    own_lane = (iota((CROWS, HALF), 1) // SUB) == (iota((CROWS, HALF), 0) % SLOT) % 4
    fold = hot(iota((SUB, HALF), 1) % SUB == iota((SUB, HALF), 0))
    first = hot(iota((HALF, HALF), 0) % SUB == 0)

    def decode(chunk):
        loop(max(chunk * CHUNK, 1), chunk * CHUNK + CHUNK, lambda d: out_copy(d).wait_recv())
        message = got[chunk * CHUNK : chunk * CHUNK + CHUNK].reshape(CMSG, HALF)
        codes = jnp.where(own_lane, nn(pick_code, message), 0.0).astype(BF16)
        rows = jnp.concatenate([nn(pick_low, message), nn(pick_high, message)], axis=1)
        code_t = nt(fold, codes)
        code_col = nn(codes, first)
        keep = [code_col > 0.0, code_col < 0.0]
        which = (jnp.abs(code_t) - 1.0).astype(I32)
        parts = [[], []]
        for s in range(SUB):
            index = jnp.broadcast_to(which[s : s + 1], (8, CROWS))
            sign = jnp.broadcast_to(code_t[s : s + 1], (8, CROWS))
            near = index & 127
            for c in range(2):
                left = table[c, 8 * s : 8 * s + 8, 0:128]
                right = table[c, 8 * s : 8 * s + 8, 128:256]
                left = jnp.take_along_axis(left, near, axis=1, mode="promise_in_bounds")
                right = jnp.take_along_axis(right, near, axis=1, mode="promise_in_bounds")
                value = jnp.where(index < 128, left, right)
                valid = sign > 0.0 if c == 0 else sign < 0.0
                parts[c].append(jnp.where(valid, value, 0.0))
        rebuilt_t = [jnp.concatenate(p, axis=0) for p in parts]
        rebuilt[chunk] = (rebuilt_t[0] + rebuilt_t[1]).T
        for c in range(2):
            residual = (rows - cent[c : c + 1]).astype(BF16)
            cov[c] += nn(rebuilt_t[c].astype(BF16), residual)
            both = jnp.concatenate([keep[c], keep[c]], axis=1)
            resid[c, chunk] = jnp.where(both, residual.astype(F32), 0.0).astype(BF16)

    for chunk in CHUNK_ORDER:
        decode(chunk)

    polar = []
    for c in range(2):
        norm = jnp.sum(cov[c] * cov[c], keepdims=True)
        polar.append(cov[c] * lax.rsqrt(norm + 1e-06))
    for _ in range(NEWTON):
        small = [q.astype(BF16) for q in polar]
        gram = [nt(q, q).astype(BF16) for q in small]
        polar = [1.5 * q - 0.5 * nn(g, b) for q, g, b in zip(polar, gram, small)]
    turn = [q.astype(BF16) for q in polar]

    total = jnp.zeros((1, D), F32)
    for chunk in range(CHUNKS):
        turned = nt(resid[0, chunk], turn[0]) + nt(resid[1, chunk], turn[1])
        off = turned - rebuilt[chunk]
        back[chunk * CHUNK : chunk * CHUNK + CHUNK] = turned.astype(BF16).reshape(CHUNK, SLOT, D)
        total = total + jnp.sum(off * off, axis=0, keepdims=True)
    err_mine[...] = total[:, :HALF] + total[:, HALF:]

    def grp_copy(step):
        return pltpu.make_async_remote_copy(
            src_ref=err_mine,
            dst_ref=err_grp.at[step],
            send_sem=eg_out.at[step],
            recv_sem=eg_in.at[step],
            device_id=level(step),
            device_id_type=MESH,
        )

    def back_copy(delta):
        return pltpu.make_async_remote_copy(
            src_ref=back.at[delta],
            dst_ref=ret.at[delta],
            send_sem=back_sem.at[delta],
            recv_sem=ret_sem.at[delta],
            device_id=behind(delta),
            device_id_type=MESH,
        )

    def peer_copy(delta):
        return pltpu.make_async_remote_copy(
            src_ref=err_sum,
            dst_ref=err_peer.at[delta],
            send_sem=ep_out.at[delta],
            recv_sem=ep_in.at[delta],
            device_id=ahead(delta),
            device_id_type=MESH,
        )

    for step in levels:
        grp_copy(step).start()
    for delta in FAR_FIRST:
        back_copy(delta).start()
    err_grp[0] = err_mine[...]
    ret[0] = back[0]
    for c in range(2):
        rot_ref[c] = polar[c].T

    loop(1, groups, lambda s: grp_copy(s).wait_recv())
    err_sum[...] = jnp.sum(err_grp[...], axis=0)
    for delta in FAR_FIRST:
        peer_copy(delta).start()
    err_peer[0] = err_sum[...]

    loop(1, PEERS, lambda d: back_copy(d).wait_recv())
    rotated_ref[...] = nn(perm_t[...], ret[...].reshape(PEERS * SLOT, D)).astype(BF16)

    loop(1, PEERS, lambda d: out_copy(d).wait_send())
    loop(1, PEERS, lambda d: back_copy(d).wait_send())
    loop(1, groups, lambda s: grp_copy(s).wait_send())
    loop(1, PEERS, lambda d: peer_copy(d).wait_recv())
    sums = jnp.sum(err_peer[...], axis=0)
    scale = 1.0 / (ROWS_DEV * PEERS * groups * D)
    dist_ref[...] = jnp.sum(sums, axis=1, keepdims=True) * scale
    loop(1, PEERS, lambda d: peer_copy(d).wait_send())


def solution(mesh):
    groups = mesh.shape["grp"]
    vmem = pl.BlockSpec(memory_space=pltpu.VMEM)
    hbm = pl.BlockSpec(memory_space=pltpu.HBM)

    def local(descriptors, cell_ids, sub_codes, centroids, codebooks):
        operands = (
            descriptors,
            cell_ids.reshape(1, ROWS_DEV),
            sub_codes.T,
            centroids,
            codebooks,
        )
        rotated, rotations, distortion = pl.pallas_call(
            lambda *refs: kernel(groups, *refs),
            out_shape=(
                pltpu.VMEM((ROWS_DEV, D), BF16),
                pltpu.VMEM((2, D, D), F32),
                jax.ShapeDtypeStruct((1, 1), F32),
            ),
            in_specs=[hbm] * 5,
            out_specs=(vmem,) * 3,
            scratch_shapes=[
                pltpu.VMEM((ROWS_DEV, D), BF16),
                pltpu.VMEM((1, ROWS_DEV), I32),
                pltpu.VMEM((SUB, ROWS_DEV), I32),
                pltpu.VMEM((2, D), BF16),
                pltpu.VMEM((2, CODES, D), BF16),
                pltpu.SemaphoreType.DMA((5,)),
                pltpu.VMEM((PEERS, MSG, HALF), BF16),
                pltpu.VMEM((PEERS, MSG, HALF), BF16),
                pltpu.VMEM((PEERS, SLOT, D), BF16),
                pltpu.VMEM((PEERS, SLOT, D), BF16),
                pltpu.VMEM((2, D, CODES), F32),
                pltpu.VMEM((CHUNKS, CROWS, D), F32),
                pltpu.VMEM((2, CHUNKS, CROWS, D), BF16),
                pltpu.VMEM((2, D, D), F32),
                pltpu.VMEM((ROWS_DEV, PEERS * SLOT), BF16),
                pltpu.VMEM((1, HALF), F32),
                pltpu.VMEM((groups, 1, HALF), F32),
                pltpu.VMEM((1, HALF), F32),
                pltpu.VMEM((PEERS, 1, HALF), F32),
                pltpu.SemaphoreType.DMA((PEERS,)),
                pltpu.SemaphoreType.DMA((PEERS,)),
                pltpu.SemaphoreType.DMA((PEERS,)),
                pltpu.SemaphoreType.DMA((PEERS,)),
                pltpu.SemaphoreType.DMA((groups,)),
                pltpu.SemaphoreType.DMA((groups,)),
                pltpu.SemaphoreType.DMA((PEERS,)),
                pltpu.SemaphoreType.DMA((PEERS,)),
            ],
            compiler_params=pltpu.CompilerParams(
                collective_id=0, has_side_effects=True, vmem_limit_bytes=32 * 1024 * 1024
            ),
        )(*(pltpu.with_memory_space_constraint(x, pltpu.HBM) for x in operands))
        return rotated, rotations, distortion.reshape(())

    rows = P(("grp", "peer"), None)
    cells = P(("grp", "peer"), None, None)
    return jax.shard_map(
        local,
        mesh=mesh,
        in_specs=(rows, P(("grp", "peer")), rows, rows, cells),
        out_specs=(rows, cells, P()),
        check_vma=False,
    )
```

time: 57.2 us -> 48.2 us (0.84)
  Pallas kernels: 49.8 us -> 44.3 us
  local copies, waits for them, and re-layouts: 4.74 us -> 1.45 us
    pallas_call x1, Pallas kernels: 49.8 us -> 44.3 us  [local(): pl.pallas_call(lambda *refs: kernel(groups, *refs), out_shape=(pltpu.VMEM...]
    unnamed x12 -> x2, local copies, waits for them, and re-layouts: 4.74 us -> 1.45 us
where the time goes in v2:
time: 48.2 us; the launch traced here: 48 us
  Pallas kernels  44.3 us (92%)
  between operations  2.33 us (5%)
  local copies, waits for them, and re-layouts  1.45 us (3%)
    pallas_call x1, Pallas kernels, local(): pl.pallas_call(lambda *refs: kernel(groups, *refs), out_shape=(pltpu.VMEM...  44.3 us
    unnamed x2, local copies, waits for them, and re-layouts  1.45 us

profile of v2, /device:TPU:1, one launch (start us, length us, event | category | flops | bytes accessed | tf_op | source)
XLA Modules:
  0.0 48.0 jit_solution(17947122063174117969)
XLA Ops:
  0.6 44.3 %shard_map.76 = (bf16[256,256]{1,0:T(8,128)(2,1)S(1)}, f32[2,256,256]{2,1,0:T(8,128)S(1)}, f32[1,1]{1,0:T(1,128)}) custom-call(bf16[256,256]{1,0:T(8,128)(2,1)} %refs_0_.1, s32[1,256]{1,0:T(1,128)} %bitcast.4, s32[32,256]{1,0:T(8,128)} %bitcast.3, bf16[2,256]{1,0:T(2,128)(2,1)} %refs_3_.1, bf16[2,256,256]{2,1,0:T(8,128)(2,1)} %refs_4_.1), custom_call_target="tpu_custom_call" | custom-call | tf_op jit(solution)/shard_map/pallas_call | solution.py:321
  44.9 0.7 %copy.11 = bf16[256,256]{1,0:T(8,128)(2,1)} copy(bf16[256,256]{1,0:T(8,128)(2,1)S(1)} %get-tuple-element.9) | data formatting | bytes 262144
  45.6 0.8 %copy.12 = f32[2,256,256]{2,1,0:T(8,128)} copy(f32[2,256,256]{2,1,0:T(8,128)S(1)} %get-tuple-element.10) | data formatting | bytes 1048576

commit v3 on v2

--- a/solution.py
+++ b/solution.py
@@ -49,12 +49,8 @@
     return mask.astype(F32).astype(BF16)
 
 
-def loop(start, stop, act):
-    def body(index, carry):
-        act(index)
-        return carry
-
-    lax.fori_loop(start, stop, body, 0)
+def drain(ref, sem):
+    pltpu.make_async_copy(ref, ref, sem.at[0]).wait()
 
 
 def kernel(
@@ -80,7 +76,7 @@
     table,
     rebuilt,
     resid,
-    cov,
+    decoded,
     perm_t,
     err_mine,
     err_grp,
@@ -113,12 +109,6 @@
     def level(step):
         return ((me_g + step) % groups, me_p)
 
-    barrier = pltpu.get_barrier_semaphore()
-    for delta in FAR_FIRST:
-        pl.semaphore_signal(barrier, inc=1, device_id=ahead(delta), device_id_type=MESH)
-    for step in levels:
-        pl.semaphore_signal(barrier, inc=1, device_id=level(step), device_id_type=MESH)
-
     loads = [
         pltpu.make_async_copy(src, dst, load_sem.at[i])
         for i, (src, dst) in enumerate(
@@ -133,6 +123,12 @@
     ]
     for load in loads:
         load.start()
+
+    barrier = pltpu.get_barrier_semaphore()
+    for delta in FAR_FIRST:
+        pl.semaphore_signal(barrier, inc=1, device_id=ahead(delta), device_id_type=MESH)
+    for step in levels:
+        pl.semaphore_signal(barrier, inc=1, device_id=level(step), device_id_type=MESH)
 
     loads[0].wait()
     cell = cell_ref[...]
@@ -164,8 +160,8 @@
         return pltpu.make_async_remote_copy(
             src_ref=send.at[delta],
             dst_ref=got.at[delta],
-            send_sem=out_sem.at[delta],
-            recv_sem=in_sem.at[delta],
+            send_sem=out_sem.at[0],
+            recv_sem=in_sem.at[delta // CHUNK],
             device_id=ahead(delta),
             device_id_type=MESH,
         )
@@ -181,7 +177,6 @@
     loads[4].wait()
     for c in range(2):
         table[c] = book_ref[c].astype(F32).T
-    cov[...] = jnp.zeros_like(cov)
     cent = cent_ref[...].astype(F32)
 
     row = iota((CROWS, CMSG), 0)
@@ -197,7 +192,8 @@
     first = hot(iota((HALF, HALF), 0) % SUB == 0)
 
     def decode(chunk):
-        loop(max(chunk * CHUNK, 1), chunk * CHUNK + CHUNK, lambda d: out_copy(d).wait_recv())
+        arrived = got.at[max(chunk * CHUNK, 1) : chunk * CHUNK + CHUNK]
+        pltpu.make_async_copy(arrived, arrived, in_sem.at[chunk]).wait()
         message = got[chunk * CHUNK : chunk * CHUNK + CHUNK].reshape(CMSG, HALF)
         codes = jnp.where(own_lane, nn(pick_code, message), 0.0).astype(BF16)
         rows = jnp.concatenate([nn(pick_low, message), nn(pick_high, message)], axis=1)
@@ -219,40 +215,39 @@
                 valid = sign > 0.0 if c == 0 else sign < 0.0
                 parts[c].append(jnp.where(valid, value, 0.0))
         rebuilt_t = [jnp.concatenate(p, axis=0) for p in parts]
-        rebuilt[chunk] = (rebuilt_t[0] + rebuilt_t[1]).T
+        here = slice(chunk * CROWS, chunk * CROWS + CROWS)
+        rebuilt[here] = (rebuilt_t[0] + rebuilt_t[1]).T
         for c in range(2):
-            residual = (rows - cent[c : c + 1]).astype(BF16)
-            cov[c] += nn(rebuilt_t[c].astype(BF16), residual)
             both = jnp.concatenate([keep[c], keep[c]], axis=1)
-            resid[c, chunk] = jnp.where(both, residual.astype(F32), 0.0).astype(BF16)
+            resid[c, here] = jnp.where(both, rows - cent[c : c + 1], 0.0).astype(BF16)
+            decoded[c, :, here] = rebuilt_t[c].astype(BF16)
 
     for chunk in CHUNK_ORDER:
         decode(chunk)
 
-    polar = []
-    for c in range(2):
-        norm = jnp.sum(cov[c] * cov[c], keepdims=True)
-        polar.append(cov[c] * lax.rsqrt(norm + 1e-06))
-    for _ in range(NEWTON):
+    cov = [nn(decoded[c], resid[c]) for c in range(2)]
+    inverse = [lax.rsqrt(jnp.sum(m * m, keepdims=True) + 1e-06) for m in cov]
+    small = [m.astype(BF16) for m in cov]
+    gram = [(nt(b, b) * (i * i)).astype(BF16) for b, i in zip(small, inverse)]
+    polar = [i * (1.5 * m - 0.5 * nn(g, b)) for m, g, b, i in zip(cov, gram, small, inverse)]
+    for _ in range(NEWTON - 1):
         small = [q.astype(BF16) for q in polar]
-        gram = [nt(q, q).astype(BF16) for q in small]
+        gram = [nt(b, b).astype(BF16) for b in small]
         polar = [1.5 * q - 0.5 * nn(g, b) for q, g, b in zip(polar, gram, small)]
     turn = [q.astype(BF16) for q in polar]
 
-    total = jnp.zeros((1, D), F32)
-    for chunk in range(CHUNKS):
-        turned = nt(resid[0, chunk], turn[0]) + nt(resid[1, chunk], turn[1])
-        off = turned - rebuilt[chunk]
-        back[chunk * CHUNK : chunk * CHUNK + CHUNK] = turned.astype(BF16).reshape(CHUNK, SLOT, D)
-        total = total + jnp.sum(off * off, axis=0, keepdims=True)
+    turned = nt(resid[0], turn[0]) + nt(resid[1], turn[1])
+    back[...] = turned.astype(BF16).reshape(PEERS, SLOT, D)
+    off = turned - rebuilt[...]
+    total = jnp.sum(off * off, axis=0, keepdims=True)
     err_mine[...] = total[:, :HALF] + total[:, HALF:]
 
     def grp_copy(step):
         return pltpu.make_async_remote_copy(
             src_ref=err_mine,
             dst_ref=err_grp.at[step],
-            send_sem=eg_out.at[step],
-            recv_sem=eg_in.at[step],
+            send_sem=eg_out.at[0],
+            recv_sem=eg_in.at[0],
             device_id=level(step),
             device_id_type=MESH,
         )
@@ -261,8 +256,8 @@
         return pltpu.make_async_remote_copy(
             src_ref=back.at[delta],
             dst_ref=ret.at[delta],
-            send_sem=back_sem.at[delta],
-            recv_sem=ret_sem.at[delta],
+            send_sem=back_sem.at[0],
+            recv_sem=ret_sem.at[0],
             device_id=behind(delta),
             device_id_type=MESH,
         )
@@ -271,8 +266,8 @@
         return pltpu.make_async_remote_copy(
             src_ref=err_sum,
             dst_ref=err_peer.at[delta],
-            send_sem=ep_out.at[delta],
-            recv_sem=ep_in.at[delta],
+            send_sem=ep_out.at[0],
+            recv_sem=ep_in.at[0],
             device_id=ahead(delta),
             device_id_type=MESH,
         )
@@ -285,24 +280,35 @@
     ret[0] = back[0]
     for c in range(2):
         rot_ref[c] = polar[c].T
-
-    loop(1, groups, lambda s: grp_copy(s).wait_recv())
+    drain(send.at[1:PEERS], out_sem)
+
+    drain(err_grp.at[1:groups], eg_in)
     err_sum[...] = jnp.sum(err_grp[...], axis=0)
     for delta in FAR_FIRST:
         peer_copy(delta).start()
     err_peer[0] = err_sum[...]
 
-    loop(1, PEERS, lambda d: back_copy(d).wait_recv())
+    drain(ret.at[1:PEERS], ret_sem)
     rotated_ref[...] = nn(perm_t[...], ret[...].reshape(PEERS * SLOT, D)).astype(BF16)
 
-    loop(1, PEERS, lambda d: out_copy(d).wait_send())
-    loop(1, PEERS, lambda d: back_copy(d).wait_send())
-    loop(1, groups, lambda s: grp_copy(s).wait_send())
-    loop(1, PEERS, lambda d: peer_copy(d).wait_recv())
+    drain(back.at[1:PEERS], back_sem)
+    drain(err_grp.at[1:groups], eg_out)
+    drain(err_peer.at[1:PEERS], ep_in)
     sums = jnp.sum(err_peer[...], axis=0)
     scale = 1.0 / (ROWS_DEV * PEERS * groups * D)
-    dist_ref[...] = jnp.sum(sums, axis=1, keepdims=True) * scale
-    loop(1, PEERS, lambda d: peer_copy(d).wait_send())
+    dist_ref[0, 0] = jnp.sum(sums) * scale
+    drain(err_peer.at[1:PEERS], ep_out)
+
+
+def place_results(rotated_in, rot_in, rotated_out, rot_out, sem):
+    copies = [
+        pltpu.make_async_copy(rot_in, rot_out, sem.at[0]),
+        pltpu.make_async_copy(rotated_in, rotated_out, sem.at[1]),
+    ]
+    for copy in copies:
+        copy.start()
+    for copy in copies:
+        copy.wait()
 
 
 def solution(mesh):
@@ -323,10 +329,10 @@
             out_shape=(
                 pltpu.VMEM((ROWS_DEV, D), BF16),
                 pltpu.VMEM((2, D, D), F32),
-                jax.ShapeDtypeStruct((1, 1), F32),
+                pltpu.SMEM((1, 1), F32),
             ),
             in_specs=[hbm] * 5,
-            out_specs=(vmem,) * 3,
+            out_specs=(vmem, vmem, pl.BlockSpec(memory_space=pltpu.SMEM)),
             scratch_shapes=[
                 pltpu.VMEM((ROWS_DEV, D), BF16),
                 pltpu.VMEM((1, ROWS_DEV), I32),
@@ -339,27 +345,35 @@
                 pltpu.VMEM((PEERS, SLOT, D), BF16),
                 pltpu.VMEM((PEERS, SLOT, D), BF16),
                 pltpu.VMEM((2, D, CODES), F32),
-                pltpu.VMEM((CHUNKS, CROWS, D), F32),
-                pltpu.VMEM((2, CHUNKS, CROWS, D), BF16),
-                pltpu.VMEM((2, D, D), F32),
+                pltpu.VMEM((PEERS * SLOT, D), F32),
+                pltpu.VMEM((2, PEERS * SLOT, D), BF16),
+                pltpu.VMEM((2, D, PEERS * SLOT), BF16),
                 pltpu.VMEM((ROWS_DEV, PEERS * SLOT), BF16),
                 pltpu.VMEM((1, HALF), F32),
                 pltpu.VMEM((groups, 1, HALF), F32),
                 pltpu.VMEM((1, HALF), F32),
                 pltpu.VMEM((PEERS, 1, HALF), F32),
-                pltpu.SemaphoreType.DMA((PEERS,)),
-                pltpu.SemaphoreType.DMA((PEERS,)),
-                pltpu.SemaphoreType.DMA((PEERS,)),
-                pltpu.SemaphoreType.DMA((PEERS,)),
-                pltpu.SemaphoreType.DMA((groups,)),
-                pltpu.SemaphoreType.DMA((groups,)),
-                pltpu.SemaphoreType.DMA((PEERS,)),
-                pltpu.SemaphoreType.DMA((PEERS,)),
+                pltpu.SemaphoreType.DMA((1,)),
+                pltpu.SemaphoreType.DMA((CHUNKS,)),
+                pltpu.SemaphoreType.DMA((1,)),
+                pltpu.SemaphoreType.DMA((1,)),
+                pltpu.SemaphoreType.DMA((1,)),
+                pltpu.SemaphoreType.DMA((1,)),
+                pltpu.SemaphoreType.DMA((1,)),
+                pltpu.SemaphoreType.DMA((1,)),
             ],
             compiler_params=pltpu.CompilerParams(
                 collective_id=0, has_side_effects=True, vmem_limit_bytes=32 * 1024 * 1024
             ),
         )(*(pltpu.with_memory_space_constraint(x, pltpu.HBM) for x in operands))
+        rotated, rotations = pl.pallas_call(
+            place_results,
+            out_shape=(pltpu.HBM((ROWS_DEV, D), BF16), pltpu.HBM((2, D, D), F32)),
+            in_specs=[pl.BlockSpec(memory_space=pl.ANY)] * 2,
+            out_specs=(hbm, hbm),
+            scratch_shapes=[pltpu.SemaphoreType.DMA((2,))],
+            compiler_params=pltpu.CompilerParams(vmem_limit_bytes=1024 * 1024),
+        )(rotated, rotations)
         return rotated, rotations, distortion.reshape(())
 
     rows = P(("grp", "peer"), None)

time: 48.2 us -> 43.6 us (0.905)
  Pallas kernels: 44.3 us -> 42.3 us
  local copies, waits for them, and re-layouts: 1.45 us -> 0 us
  between operations: 2.33 us -> 1.16 us
    pallas_call x1, Pallas kernels: 44.3 us -> 41.5 us  [local(): pl.pallas_call(lambda *refs: kernel(groups, *refs), out_shape=(pltpu.VMEM...]
    unnamed x2 -> x0, local copies, waits for them, and re-layouts: 1.45 us -> none
    pallas_call x0 -> x1, Pallas kernels: none -> 0.85 us  [local(): pl.pallas_call(place_results, out_shape=(pltpu.HBM((ROWS_DEV, D), BF16),...]
where the time goes in v3:
time: 43.6 us; the launch traced here: 43.5 us
  Pallas kernels  42.3 us (97%)
  between operations  1.16 us (3%)
    pallas_call x1, Pallas kernels, local(): pl.pallas_call(lambda *refs: kernel(groups, *refs), out_shape=(pltpu.VMEM...  41.5 us

profile of v3, /device:TPU:1, one launch (start us, length us, event | category | flops | bytes accessed | tf_op | source)
XLA Modules:
  0.0 43.5 jit_solution(13223004235244884170)
XLA Ops:
  0.6 41.5 %shard_map.76 = (bf16[256,256]{1,0:T(8,128)(2,1)S(1)}, f32[2,256,256]{2,1,0:T(8,128)S(1)}, f32[1,1]{1,0:T(1,128)S(4)}) custom-call(bf16[256,256]{1,0:T(8,128)(2,1)} %refs_0_.1, s32[1,256]{1,0:T(1,128)} %bitcast.4, s32[32,256]{1,0:T(8,128)} %bitcast.3, bf16[2,256]{1,0:T(2,128)(2,1)} %refs_3_.1, bf16[2,256,256]{2,1,0:T(8,128)(2,1)} %refs_4_.1), custom_call_target="tpu_custom_call" | custom-call | tf_op jit(solution)/shard_map/pallas_call | solution.py:327
  42.6 0.8 %shard_map.77 = (bf16[256,256]{1,0:T(8,128)(2,1)}, f32[2,256,256]{2,1,0:T(8,128)}) custom-call(bf16[256,256]{1,0:T(8,128)(2,1)S(1)} %get-tuple-element.8.rotated_in, f32[2,256,256]{2,1,0:T(8,128)S(1)} %get-tuple-element.9.rot_in), custom_call_target="tpu_custom_call" | custom-call | tf_op jit(solution)/shard_map/pallas_call | solution.py:369

commit v4 on v3

--- a/solution.py
+++ b/solution.py
@@ -19,6 +19,8 @@
 SLOT = 16
 CHUNK = 8
 CHUNKS = PEERS // CHUNK
+CORES = 2
+HUB_PLANES = 4
 CROWS = CHUNK * SLOT
 CMSG = CHUNK * MSG
 F32, BF16, I32 = jnp.float32, jnp.bfloat16, jnp.int32
@@ -30,7 +32,7 @@
 
 
 FAR_FIRST = sorted(range(1, PEERS), key=lambda delta: -hops(delta))
-CHUNK_ORDER = (2, 1, 3, 0)
+CHUNK_ORDER = ((2, 1, 3, 0),)
 
 
 def nn(a, b):
@@ -82,6 +84,7 @@
     err_grp,
     err_sum,
     err_peer,
+    err_total,
     out_sem,
     in_sem,
     back_sem,
@@ -90,11 +93,18 @@
     eg_in,
     ep_out,
     ep_in,
+    et_out,
+    et_in,
 ):
     me_g = lax.axis_index("grp")
     me_p = lax.axis_index("peer")
     my_y, my_x = me_p // X_SIZE, me_p % X_SIZE
-    levels = sorted(range(1, groups), key=lambda step: abs(2 * step - groups))
+    core, plane = me_g % CORES, me_g // CORES
+    hubs = min(HUB_PLANES * CORES, groups)
+    far = range(HUB_PLANES, groups // CORES)
+    is_hub = me_g < hubs
+    is_relay = plane == HUB_PLANES - 1
+    greeted = PEERS - 1 + jnp.where(is_hub, hubs - 1, hubs) + jnp.where(is_relay, len(far), 0)
 
     def ahead(delta):
         to_y = (my_y + delta // X_SIZE) % Y_SIZE
@@ -127,8 +137,16 @@
     barrier = pltpu.get_barrier_semaphore()
     for delta in FAR_FIRST:
         pl.semaphore_signal(barrier, inc=1, device_id=ahead(delta), device_id_type=MESH)
-    for step in levels:
-        pl.semaphore_signal(barrier, inc=1, device_id=level(step), device_id_type=MESH)
+
+    @pl.when(is_hub)
+    def _():
+        for step in range(1, groups):
+            pl.semaphore_signal(barrier, inc=1, device_id=level(step), device_id_type=MESH)
+
+    @pl.when(jnp.logical_not(is_hub))
+    def _():
+        relay = ((HUB_PLANES - 1) * CORES + core, me_p)
+        pl.semaphore_signal(barrier, inc=1, device_id=relay, device_id_type=MESH)
 
     loads[0].wait()
     cell = cell_ref[...]
@@ -154,7 +172,7 @@
     )
     send[...] = packed.astype(BF16).reshape(PEERS, MSG, HALF)
 
-    pl.semaphore_wait(barrier, PEERS - 1 + groups - 1)
+    pl.semaphore_wait(barrier, greeted)
 
     def out_copy(delta):
         return pltpu.make_async_remote_copy(
@@ -191,39 +209,48 @@
     fold = hot(iota((SUB, HALF), 1) % SUB == iota((SUB, HALF), 0))
     first = hot(iota((HALF, HALF), 0) % SUB == 0)
 
-    def decode(chunk):
-        arrived = got.at[max(chunk * CHUNK, 1) : chunk * CHUNK + CHUNK]
-        pltpu.make_async_copy(arrived, arrived, in_sem.at[chunk]).wait()
-        message = got[chunk * CHUNK : chunk * CHUNK + CHUNK].reshape(CMSG, HALF)
-        codes = jnp.where(own_lane, nn(pick_code, message), 0.0).astype(BF16)
-        rows = jnp.concatenate([nn(pick_low, message), nn(pick_high, message)], axis=1)
-        code_t = nt(fold, codes)
-        code_col = nn(codes, first)
-        keep = [code_col > 0.0, code_col < 0.0]
-        which = (jnp.abs(code_t) - 1.0).astype(I32)
-        parts = [[], []]
-        for s in range(SUB):
-            index = jnp.broadcast_to(which[s : s + 1], (8, CROWS))
-            sign = jnp.broadcast_to(code_t[s : s + 1], (8, CROWS))
-            near = index & 127
+    def decode(chunks):
+        messages = []
+        for chunk in chunks:
+            arrived = got.at[max(chunk * CHUNK, 1) : chunk * CHUNK + CHUNK]
+            pltpu.make_async_copy(arrived, arrived, in_sem.at[chunk]).wait()
+        for chunk in chunks:
+            message = got[chunk * CHUNK : chunk * CHUNK + CHUNK].reshape(CMSG, HALF)
+            messages.append(message)
+        codes = [jnp.where(own_lane, nn(pick_code, m), 0.0).astype(BF16) for m in messages]
+        code_ts = [nt(fold, x) for x in codes]
+        code_cols = [nn(x, first) for x in codes]
+        for chunk, message, code_t, code_col in zip(chunks, messages, code_ts, code_cols):
+            here = slice(chunk * CROWS, chunk * CROWS + CROWS)
+            which = (jnp.abs(code_t) - 1.0).astype(I32)
+            parts = [[], []]
+            for s in range(SUB):
+                index = jnp.broadcast_to(which[s : s + 1], (8, CROWS))
+                sign = jnp.broadcast_to(code_t[s : s + 1], (8, CROWS))
+                near = index & 127
+                part = slice(8 * s, 8 * s + 8)
+                values = []
+                for c in range(2):
+                    left = table[c, part, 0:128]
+                    right = table[c, part, 128:256]
+                    left = jnp.take_along_axis(left, near, axis=1, mode="promise_in_bounds")
+                    right = jnp.take_along_axis(right, near, axis=1, mode="promise_in_bounds")
+                    value = jnp.where(index < 128, left, right)
+                    valid = sign > 0.0 if c == 0 else sign < 0.0
+                    values.append(jnp.where(valid, value, 0.0))
+                    parts[c].append(values[c])
+            rebuilt_t = [jnp.concatenate(p, axis=0) for p in parts]
             for c in range(2):
-                left = table[c, 8 * s : 8 * s + 8, 0:128]
-                right = table[c, 8 * s : 8 * s + 8, 128:256]
-                left = jnp.take_along_axis(left, near, axis=1, mode="promise_in_bounds")
-                right = jnp.take_along_axis(right, near, axis=1, mode="promise_in_bounds")
-                value = jnp.where(index < 128, left, right)
-                valid = sign > 0.0 if c == 0 else sign < 0.0
-                parts[c].append(jnp.where(valid, value, 0.0))
-        rebuilt_t = [jnp.concatenate(p, axis=0) for p in parts]
-        here = slice(chunk * CROWS, chunk * CROWS + CROWS)
-        rebuilt[here] = (rebuilt_t[0] + rebuilt_t[1]).T
-        for c in range(2):
-            both = jnp.concatenate([keep[c], keep[c]], axis=1)
-            resid[c, here] = jnp.where(both, rows - cent[c : c + 1], 0.0).astype(BF16)
-            decoded[c, :, here] = rebuilt_t[c].astype(BF16)
-
-    for chunk in CHUNK_ORDER:
-        decode(chunk)
+                decoded[c, :, here] = rebuilt_t[c].astype(BF16)
+            rebuilt[here] = (rebuilt_t[0] + rebuilt_t[1]).T
+            rows = jnp.concatenate([nn(pick_low, message), nn(pick_high, message)], axis=1)
+            keep = [code_col > 0.0, code_col < 0.0]
+            for c in range(2):
+                both = jnp.concatenate([keep[c], keep[c]], axis=1)
+                resid[c, here] = jnp.where(both, rows - cent[c : c + 1], 0.0).astype(BF16)
+
+    for chunks in CHUNK_ORDER:
+        decode(chunks)
 
     cov = [nn(decoded[c], resid[c]) for c in range(2)]
     inverse = [lax.rsqrt(jnp.sum(m * m, keepdims=True) + 1e-06) for m in cov]
@@ -237,18 +264,27 @@
     turn = [q.astype(BF16) for q in polar]
 
     turned = nt(resid[0], turn[0]) + nt(resid[1], turn[1])
-    back[...] = turned.astype(BF16).reshape(PEERS, SLOT, D)
     off = turned - rebuilt[...]
     total = jnp.sum(off * off, axis=0, keepdims=True)
     err_mine[...] = total[:, :HALF] + total[:, HALF:]
 
-    def grp_copy(step):
+    def hub_copy(hub):
         return pltpu.make_async_remote_copy(
             src_ref=err_mine,
-            dst_ref=err_grp.at[step],
+            dst_ref=err_grp.at[(me_g + groups - hub) % groups],
             send_sem=eg_out.at[0],
             recv_sem=eg_in.at[0],
-            device_id=level(step),
+            device_id=(hub, me_p),
+            device_id_type=MESH,
+        )
+
+    def total_copy(to_plane):
+        return pltpu.make_async_remote_copy(
+            src_ref=err_total,
+            dst_ref=err_total,
+            send_sem=et_out.at[0],
+            recv_sem=et_in.at[0],
+            device_id=(to_plane * CORES + core, me_p),
             device_id_type=MESH,
         )
 
@@ -272,8 +308,13 @@
             device_id_type=MESH,
         )
 
-    for step in levels:
-        grp_copy(step).start()
+    for hub in range(hubs):
+
+        @pl.when(me_g != hub)
+        def _():
+            hub_copy(hub).start()
+
+    back[...] = turned.astype(BF16).reshape(PEERS, SLOT, D)
     for delta in FAR_FIRST:
         back_copy(delta).start()
     err_grp[0] = err_mine[...]
@@ -282,22 +323,48 @@
         rot_ref[c] = polar[c].T
     drain(send.at[1:PEERS], out_sem)
 
-    drain(err_grp.at[1:groups], eg_in)
-    err_sum[...] = jnp.sum(err_grp[...], axis=0)
-    for delta in FAR_FIRST:
-        peer_copy(delta).start()
-    err_peer[0] = err_sum[...]
+    @pl.when(is_hub)
+    def _():
+        drain(err_grp.at[1:groups], eg_in)
+        err_sum[...] = jnp.sum(err_grp[...], axis=0)
+        for delta in FAR_FIRST:
+            peer_copy(delta).start()
+        err_peer[0] = err_sum[...]
+        drain(err_grp.at[1:hubs], eg_out)
+
+    @pl.when(jnp.logical_not(is_hub))
+    def _():
+        drain(err_grp.at[0:hubs], eg_out)
 
     drain(ret.at[1:PEERS], ret_sem)
     rotated_ref[...] = nn(perm_t[...], ret[...].reshape(PEERS * SLOT, D)).astype(BF16)
-
     drain(back.at[1:PEERS], back_sem)
-    drain(err_grp.at[1:groups], eg_out)
-    drain(err_peer.at[1:PEERS], ep_in)
-    sums = jnp.sum(err_peer[...], axis=0)
+
+    @pl.when(is_hub)
+    def _():
+        drain(err_peer.at[1:PEERS], ep_in)
+        err_total[...] = jnp.sum(err_peer[...], axis=0)
+        drain(err_peer.at[1:PEERS], ep_out)
+
+    if far:
+
+        @pl.when(is_relay)
+        def _():
+            for to_plane in far:
+                total_copy(to_plane).start()
+
+        @pl.when(jnp.logical_not(is_hub))
+        def _():
+            drain(err_total, et_in)
+
     scale = 1.0 / (ROWS_DEV * PEERS * groups * D)
-    dist_ref[0, 0] = jnp.sum(sums) * scale
-    drain(err_peer.at[1:PEERS], ep_out)
+    dist_ref[0, 0] = jnp.sum(err_total[...]) * scale
+
+    if far:
+
+        @pl.when(is_relay)
+        def _():
+            drain(err_grp.at[0 : len(far)], et_out)
 
 
 def place_results(rotated_in, rot_in, rotated_out, rot_out, sem):
@@ -353,8 +420,11 @@
                 pltpu.VMEM((groups, 1, HALF), F32),
                 pltpu.VMEM((1, HALF), F32),
                 pltpu.VMEM((PEERS, 1, HALF), F32),
+                pltpu.VMEM((1, HALF), F32),
                 pltpu.SemaphoreType.DMA((1,)),
                 pltpu.SemaphoreType.DMA((CHUNKS,)),
+                pltpu.SemaphoreType.DMA((1,)),
+                pltpu.SemaphoreType.DMA((1,)),
                 pltpu.SemaphoreType.DMA((1,)),
                 pltpu.SemaphoreType.DMA((1,)),
                 pltpu.SemaphoreType.DMA((1,)),

time: 43.6 us -> 42.5 us (0.975)
  Pallas kernels: 42.3 us -> 41.2 us
    pallas_call x1, Pallas kernels: 41.5 us -> 40.3 us  [local(): pl.pallas_call(lambda *refs: kernel(groups, *refs), out_shape=(pltpu.VMEM...]
where the time goes in v4:
time: 42.5 us; the launch traced here: 42.3 us
  Pallas kernels  41.2 us (97%)
  between operations  1.16 us (3%)
    pallas_call x1, Pallas kernels, local(): pl.pallas_call(lambda *refs: kernel(groups, *refs), out_shape=(pltpu.VMEM...  40.3 us

profile of v4, /device:TPU:1, one launch (start us, length us, event | category | flops | bytes accessed | tf_op | source)
XLA Modules:
  0.0 42.3 jit_solution(4410773173661345190)
XLA Ops:
  0.6 40.3 %shard_map.76 = (bf16[256,256]{1,0:T(8,128)(2,1)S(1)}, f32[2,256,256]{2,1,0:T(8,128)S(1)}, f32[1,1]{1,0:T(1,128)S(4)}) custom-call(bf16[256,256]{1,0:T(8,128)(2,1)} %refs_0_.1, s32[1,256]{1,0:T(1,128)} %bitcast.4, s32[32,256]{1,0:T(8,128)} %bitcast.3, bf16[2,256]{1,0:T(2,128)(2,1)} %refs_3_.1, bf16[2,256,256]{2,1,0:T(8,128)(2,1)} %refs_4_.1), custom_call_target="tpu_custom_call" | custom-call | tf_op jit(solution)/shard_map/pallas_call | solution.py:394
  41.5 0.8 %shard_map.77 = (bf16[256,256]{1,0:T(8,128)(2,1)}, f32[2,256,256]{2,1,0:T(8,128)}) custom-call(bf16[256,256]{1,0:T(8,128)(2,1)S(1)} %get-tuple-element.8.rotated_in, f32[2,256,256]{2,1,0:T(8,128)S(1)} %get-tuple-element.9.rot_in), custom_call_target="tpu_custom_call" | custom-call | tf_op jit(solution)/shard_map/pallas_call | solution.py:439

commit v5 on v4

--- a/solution.py
+++ b/solution.py
@@ -247,12 +247,12 @@
             keep = [code_col > 0.0, code_col < 0.0]
             for c in range(2):
                 both = jnp.concatenate([keep[c], keep[c]], axis=1)
-                resid[c, here] = jnp.where(both, rows - cent[c : c + 1], 0.0).astype(BF16)
+                resid[here, c * D : c * D + D] = jnp.where(both, rows - cent[c : c + 1], 0.0).astype(BF16)
 
     for chunks in CHUNK_ORDER:
         decode(chunks)
 
-    cov = [nn(decoded[c], resid[c]) for c in range(2)]
+    cov = [nn(decoded[c], resid[:, c * D : c * D + D]) for c in range(2)]
     inverse = [lax.rsqrt(jnp.sum(m * m, keepdims=True) + 1e-06) for m in cov]
     small = [m.astype(BF16) for m in cov]
     gram = [(nt(b, b) * (i * i)).astype(BF16) for b, i in zip(small, inverse)]
@@ -263,7 +263,7 @@
         polar = [1.5 * q - 0.5 * nn(g, b) for q, g, b in zip(polar, gram, small)]
     turn = [q.astype(BF16) for q in polar]
 
-    turned = nt(resid[0], turn[0]) + nt(resid[1], turn[1])
+    turned = nt(resid[...], jnp.concatenate(turn, axis=1))
     off = turned - rebuilt[...]
     total = jnp.sum(off * off, axis=0, keepdims=True)
     err_mine[...] = total[:, :HALF] + total[:, HALF:]
@@ -340,11 +340,15 @@
     rotated_ref[...] = nn(perm_t[...], ret[...].reshape(PEERS * SLOT, D)).astype(BF16)
     drain(back.at[1:PEERS], back_sem)
 
+    scale = 1.0 / (ROWS_DEV * PEERS * groups * D)
+
     @pl.when(is_hub)
     def _():
+        drain(err_peer.at[1:PEERS], ep_out)
         drain(err_peer.at[1:PEERS], ep_in)
-        err_total[...] = jnp.sum(err_peer[...], axis=0)
-        drain(err_peer.at[1:PEERS], ep_out)
+        total = jnp.sum(err_peer[...], axis=0)
+        dist_ref[0, 0] = jnp.sum(total) * scale
+        err_total[...] = total
 
     if far:
 
@@ -352,25 +356,20 @@
         def _():
             for to_plane in far:
                 total_copy(to_plane).start()
+            drain(err_grp.at[0 : len(far)], et_out)
 
         @pl.when(jnp.logical_not(is_hub))
         def _():
             drain(err_total, et_in)
-
-    scale = 1.0 / (ROWS_DEV * PEERS * groups * D)
-    dist_ref[0, 0] = jnp.sum(err_total[...]) * scale
-
-    if far:
-
-        @pl.when(is_relay)
-        def _():
-            drain(err_grp.at[0 : len(far)], et_out)
-
-
-def place_results(rotated_in, rot_in, rotated_out, rot_out, sem):
+            dist_ref[0, 0] = jnp.sum(err_total[...]) * scale
+
+
+def place_results(rotated_in, rot_in, dist_in, rotated_out, rot_out, dist_out, held, sem):
+    held[...] = jnp.full((1, 1), dist_in[0, 0], F32)
     copies = [
         pltpu.make_async_copy(rot_in, rot_out, sem.at[0]),
         pltpu.make_async_copy(rotated_in, rotated_out, sem.at[1]),
+        pltpu.make_async_copy(held, dist_out, sem.at[2]),
     ]
     for copy in copies:
         copy.start()
@@ -381,6 +380,7 @@
 def solution(mesh):
     groups = mesh.shape["grp"]
     vmem = pl.BlockSpec(memory_space=pltpu.VMEM)
+    smem = pl.BlockSpec(memory_space=pltpu.SMEM)
     hbm = pl.BlockSpec(memory_space=pltpu.HBM)
 
     def local(descriptors, cell_ids, sub_codes, centroids, codebooks):
@@ -399,7 +399,7 @@
                 pltpu.SMEM((1, 1), F32),
             ),
             in_specs=[hbm] * 5,
-            out_specs=(vmem, vmem, pl.BlockSpec(memory_space=pltpu.SMEM)),
+            out_specs=(vmem, vmem, smem),
             scratch_shapes=[
                 pltpu.VMEM((ROWS_DEV, D), BF16),
                 pltpu.VMEM((1, ROWS_DEV), I32),
@@ -413,7 +413,7 @@
                 pltpu.VMEM((PEERS, SLOT, D), BF16),
                 pltpu.VMEM((2, D, CODES), F32),
                 pltpu.VMEM((PEERS * SLOT, D), F32),
-                pltpu.VMEM((2, PEERS * SLOT, D), BF16),
+                pltpu.VMEM((PEERS * SLOT, 2 * D), BF16),
                 pltpu.VMEM((2, D, PEERS * SLOT), BF16),
                 pltpu.VMEM((ROWS_DEV, PEERS * SLOT), BF16),
                 pltpu.VMEM((1, HALF), F32),
@@ -436,14 +436,18 @@
                 collective_id=0, has_side_effects=True, vmem_limit_bytes=32 * 1024 * 1024
             ),
         )(*(pltpu.with_memory_space_constraint(x, pltpu.HBM) for x in operands))
-        rotated, rotations = pl.pallas_call(
+        rotated, rotations, distortion = pl.pallas_call(
             place_results,
-            out_shape=(pltpu.HBM((ROWS_DEV, D), BF16), pltpu.HBM((2, D, D), F32)),
-            in_specs=[pl.BlockSpec(memory_space=pl.ANY)] * 2,
-            out_specs=(hbm, hbm),
-            scratch_shapes=[pltpu.SemaphoreType.DMA((2,))],
+            out_shape=(
+                pltpu.HBM((ROWS_DEV, D), BF16),
+                pltpu.HBM((2, D, D), F32),
+                pltpu.HBM((1, 1), F32),
+            ),
+            in_specs=[pl.BlockSpec(memory_space=pl.ANY)] * 2 + [smem],
+            out_specs=(hbm,) * 3,
+            scratch_shapes=[pltpu.VMEM((1, 1), F32), pltpu.SemaphoreType.DMA((3,))],
             compiler_params=pltpu.CompilerParams(vmem_limit_bytes=1024 * 1024),
-        )(rotated, rotations)
+        )(rotated, rotations, distortion)
         return rotated, rotations, distortion.reshape(())
 
     rows = P(("grp", "peer"), None)

time: 42.5 us -> 41.9 us (0.986)
  between operations: 1.16 us -> 0.64 us
where the time goes in v5:
time: 41.9 us; the launch traced here: 41.7 us
  Pallas kernels  41.1 us (98%)
  between operations  0.64 us (2%)
    pallas_call x1, Pallas kernels, local(): pl.pallas_call(lambda *refs: kernel(groups, *refs), out_shape=(pltpu.VMEM...  40.2 us
    pallas_call x1, Pallas kernels, local(): pl.pallas_call(place_results, out_shape=(pltpu.HBM((ROWS_DEV, D), BF16),...  0.86 us

profile of v5, /device:TPU:1, one launch (start us, length us, event | category | flops | bytes accessed | tf_op | source)
XLA Modules:
  0.0 41.7 jit_solution(11444725104875628487)
XLA Ops:
  0.6 40.2 %shard_map.76 = (bf16[256,256]{1,0:T(8,128)(2,1)S(1)}, f32[2,256,256]{2,1,0:T(8,128)S(1)}, f32[1,1]{1,0:T(1,128)S(4)}) custom-call(bf16[256,256]{1,0:T(8,128)(2,1)} %refs_0_.1, s32[1,256]{1,0:T(1,128)} %bitcast.4, s32[32,256]{1,0:T(8,128)} %bitcast.3, bf16[2,256]{1,0:T(2,128)(2,1)} %refs_3_.1, bf16[2,256,256]{2,1,0:T(8,128)(2,1)} %refs_4_.1), custom_call_target="tpu_custom_call" | custom-call | tf_op jit(solution)/shard_map/pallas_call | solution.py:394
  40.8 0.9 %shard_map.77 = (bf16[256,256]{1,0:T(8,128)(2,1)}, f32[2,256,256]{2,1,0:T(8,128)}, f32[1,1]{1,0:T(1,128)}) custom-call(bf16[256,256]{1,0:T(8,128)(2,1)S(1)} %get-tuple-element.9.rotated_in, f32[2,256,256]{2,1,0:T(8,128)S(1)} %get-tuple-element.10.rot_in, f32[1,1]{1,0:T(1,128)S(4)} %get-tuple-element.11.dist_in), custom_call_target="tpu_custom_call" | custom-call | tf_op jit(solution)/shard_map/pallas_call | solution.py:439

commit v6 on v5

--- a/solution.py
+++ b/solution.py
@@ -17,11 +17,12 @@
 PEERS = X_SIZE * Y_SIZE
 MSG = 24
 SLOT = 16
-CHUNK = 8
-CHUNKS = PEERS // CHUNK
+CHUNK = 12
+CHUNKS = 3
 CORES = 2
 HUB_PLANES = 4
-CROWS = CHUNK * SLOT
+CROWS = 128
+ROWS = CHUNKS * CROWS
 CMSG = CHUNK * MSG
 F32, BF16, I32 = jnp.float32, jnp.bfloat16, jnp.int32
 
@@ -32,7 +33,7 @@
 
 
 FAR_FIRST = sorted(range(1, PEERS), key=lambda delta: -hops(delta))
-CHUNK_ORDER = ((2, 1, 3, 0),)
+CHUNK_ORDER = ((0, 1, 2),)
 
 
 def nn(a, b):
@@ -79,6 +80,7 @@
     rebuilt,
     resid,
     decoded,
+    spread_out,
     perm_t,
     err_mine,
     err_grp,
@@ -187,6 +189,7 @@
     for delta in FAR_FIRST:
         out_copy(delta).start()
     got[0] = send[0]
+    got[PEERS:] = jnp.zeros((CHUNKS * CHUNK - PEERS, MSG, HALF), BF16)
 
     place = rel * SLOT + rank
     place_col = jnp.broadcast_to(place.astype(F32), (8, ROWS_DEV)).T[:, :1].astype(I32)
@@ -198,21 +201,25 @@
     cent = cent_ref[...].astype(F32)
 
     row = iota((CROWS, CMSG), 0)
-    source, slot = row // SLOT, row % SLOT
+    source, slot = row // OWN, row % OWN
     col = iota((CROWS, CMSG), 1)
     col_source, col_row = col // MSG, col % MSG
-    same = (source == col_source) & (slot < OWN)
+    same = source == col_source
     pick_low = hot(same & (col_row == slot))
     pick_high = hot(same & (col_row == slot + OWN))
     pick_code = hot(same & (col_row == 2 * OWN + (slot >> 2)))
-    own_lane = (iota((CROWS, HALF), 1) // SUB) == (iota((CROWS, HALF), 0) % SLOT) % 4
+    own_lane = (iota((CROWS, HALF), 1) // SUB) == (iota((CROWS, HALF), 0) % OWN) % 4
+    target = iota((PEERS * SLOT, 1), 0)
+    partner, slot = target // SLOT, target % SLOT
+    packed_row = (partner // CHUNK) * CROWS + (partner % CHUNK) * OWN + slot
+    spread_out[...] = hot((iota((PEERS * SLOT, ROWS), 1) == packed_row) & (slot < OWN))
     fold = hot(iota((SUB, HALF), 1) % SUB == iota((SUB, HALF), 0))
     first = hot(iota((HALF, HALF), 0) % SUB == 0)
 
     def decode(chunks):
         messages = []
         for chunk in chunks:
-            arrived = got.at[max(chunk * CHUNK, 1) : chunk * CHUNK + CHUNK]
+            arrived = got.at[max(chunk * CHUNK, 1) : min(chunk * CHUNK + CHUNK, PEERS)]
             pltpu.make_async_copy(arrived, arrived, in_sem.at[chunk]).wait()
         for chunk in chunks:
             message = got[chunk * CHUNK : chunk * CHUNK + CHUNK].reshape(CMSG, HALF)
@@ -314,7 +321,7 @@
         def _():
             hub_copy(hub).start()
 
-    back[...] = turned.astype(BF16).reshape(PEERS, SLOT, D)
+    back[...] = nn(spread_out[...], turned.astype(BF16)).astype(BF16).reshape(PEERS, SLOT, D)
     for delta in FAR_FIRST:
         back_copy(delta).start()
     err_grp[0] = err_mine[...]
@@ -408,13 +415,14 @@
                 pltpu.VMEM((2, CODES, D), BF16),
                 pltpu.SemaphoreType.DMA((5,)),
                 pltpu.VMEM((PEERS, MSG, HALF), BF16),
-                pltpu.VMEM((PEERS, MSG, HALF), BF16),
+                pltpu.VMEM((CHUNKS * CHUNK, MSG, HALF), BF16),
                 pltpu.VMEM((PEERS, SLOT, D), BF16),
                 pltpu.VMEM((PEERS, SLOT, D), BF16),
                 pltpu.VMEM((2, D, CODES), F32),
-                pltpu.VMEM((PEERS * SLOT, D), F32),
-                pltpu.VMEM((PEERS * SLOT, 2 * D), BF16),
-                pltpu.VMEM((2, D, PEERS * SLOT), BF16),
+                pltpu.VMEM((ROWS, D), F32),
+                pltpu.VMEM((ROWS, 2 * D), BF16),
+                pltpu.VMEM((2, D, ROWS), BF16),
+                pltpu.VMEM((PEERS * SLOT, ROWS), BF16),
                 pltpu.VMEM((ROWS_DEV, PEERS * SLOT), BF16),
                 pltpu.VMEM((1, HALF), F32),
                 pltpu.VMEM((groups, 1, HALF), F32),

time: 41.9 us -> 41.5 us (level)
  no operation moved by 1% of the time
where the time goes in v6:
time: 41.5 us; the launch traced here: 41.4 us
  Pallas kernels  40.7 us (98%)
  between operations  0.64 us (2%)
    pallas_call x1, Pallas kernels, local(): pl.pallas_call(lambda *refs: kernel(groups, *refs), out_shape=(pltpu.VMEM...  39.9 us
    pallas_call x1, Pallas kernels, local(): pl.pallas_call(place_results, out_shape=(pltpu.HBM((ROWS_DEV, D), BF16),...  0.86 us

profile of v6, /device:TPU:1, one launch (start us, length us, event | category | flops | bytes accessed | tf_op | source)
XLA Modules:
  0.0 41.4 jit_solution(15943362168114498813)
XLA Ops:
  0.6 39.9 %shard_map.76 = (bf16[256,256]{1,0:T(8,128)(2,1)S(1)}, f32[2,256,256]{2,1,0:T(8,128)S(1)}, f32[1,1]{1,0:T(1,128)S(4)}) custom-call(bf16[256,256]{1,0:T(8,128)(2,1)} %refs_0_.1, s32[1,256]{1,0:T(1,128)} %bitcast.4, s32[32,256]{1,0:T(8,128)} %bitcast.3, bf16[2,256]{1,0:T(2,128)(2,1)} %refs_3_.1, bf16[2,256,256]{2,1,0:T(8,128)(2,1)} %refs_4_.1), custom_call_target="tpu_custom_call" | custom-call | tf_op jit(solution)/shard_map/pallas_call | solution.py:401
  40.5 0.9 %shard_map.77 = (bf16[256,256]{1,0:T(8,128)(2,1)}, f32[2,256,256]{2,1,0:T(8,128)}, f32[1,1]{1,0:T(1,128)}) custom-call(bf16[256,256]{1,0:T(8,128)(2,1)S(1)} %get-tuple-element.9.rotated_in, f32[2,256,256]{2,1,0:T(8,128)S(1)} %get-tuple-element.10.rot_in, f32[1,1]{1,0:T(1,128)S(4)} %get-tuple-element.11.dist_in), custom_call_target="tpu_custom_call" | custom-call | tf_op jit(solution)/shard_map/pallas_call | solution.py:447
